TPU v7x, 32 devices: a whole 2x2x4 slice. The times are simulated.
32 devices in a mesh: dp: 4 (over z), ctx: 8 (over y, x, core).
Axes of the slice: x: 2, y: 2, z: 4, core: 2. Of those that a mesh axis runs over, the one named last changes fastest.
Arguments:
- query_input: bfloat16 [4, 1024, 8192], P('dp', 'ctx'), may hold values from -12 to 12
- key_input: bfloat16 [4, 1024, 1024], P('dp', 'ctx'), may hold values from -12 to 12
- value_input: bfloat16 [4, 1024, 1024], P('dp', 'ctx'), may hold values from -6 to 6
- out_grad: bfloat16 [4, 1024, 8192], P('dp', 'ctx'), may hold values from -6 to 6
- query_bias: float32 [8192], replicated, may hold values from -1.75 to 1.75
- key_bias: float32 [1024], replicated, may hold values from -1.75 to 1.75
- value_bias: float32 [1024], replicated, may hold values from -1.75 to 1.75
- parents: int32 [4, 8], P('dp'), may hold values from 0 to 6, as said below
Outputs:
- attended: bfloat16 [4, 1024, 8192], P('dp', 'ctx')
- query_grad: float32 [4, 1024, 8192], P('dp', 'ctx')
- key_grad: float32 [4, 1024, 1024], P('dp', 'ctx')
- value_grad: float32 [4, 1024, 1024], P('dp', 'ctx')
- query_bias_grad: float32 [8192], replicated
- key_bias_grad: float32 [1024], replicated
- value_bias_grad: float32 [1024], replicated
Inputs may be any that keep to these rules, and one draw needn't show every extreme that they name: parents[t, 0] = 0 marks the root block; every other block's parent is an earlier block; the last block's parent is the block before it.
All inputs are finite; a program needn't handle non-finite values.
Results may differ from a plain program's by a relative error of at most 0.028.
Values may be sent and summed in bfloat16 or wider, within the bound.
A program may use at most 128 MiB of HBM per device.

v0:
```python
import functools
import math

import jax
import jax.numpy as jnp
import numpy as np
from jax import lax
from jax.experimental import pallas as pl
from jax.experimental.pallas import tpu as pltpu
from jax.sharding import PartitionSpec as P

Q_HEADS = 64
KV_HEADS = 8
HEAD = 128
GROUP = Q_HEADS // KV_HEADS
HALF = HEAD // 2
NEG_LARGE = -1e30
SCALE = HEAD ** (-0.5)
LOG2_SCALE = SCALE * math.log2(math.e)
LN2 = math.log(2.0)
MESH = pl.DeviceIdType.MESH


def tables(depths, rows):
    frequency = 1000000.0 ** (-2.0 * np.arange(HALF) / HEAD)
    places = (np.arange(depths)[:, None] * rows + np.arange(rows)[None, :]).astype(np.float64)
    angles = places[..., None] * frequency
    cosine, sine = np.cos(angles), np.sin(angles)
    flat = np.stack(
        [np.concatenate([cosine, cosine], -1), np.concatenate([-sine, sine], -1)], axis=1
    )
    turned = np.stack([cosine.transpose(0, 2, 1), sine.transpose(0, 2, 1)], axis=1)
    return flat.astype(np.float32), turned.astype(np.float32)


def nt(a, b):
    return lax.dot_general(a, b, (((1,), (1,)), ((), ())), preferred_element_type=jnp.float32)


def tn(a, b):
    return lax.dot_general(a, b, (((0,), (0,)), ((), ())), preferred_element_type=jnp.float32)


def kernel(
    ctx,
    dps,
    parents,
    q_in,
    k_in,
    v_in,
    g_in,
    q_bias,
    k_bias,
    v_bias,
    flat_table,
    turned_table,
    att_out,
    dq_out,
    dk_out,
    dv_out,
    qb_out,
    kb_out,
    vb_out,
    negs,
    flat,
    turned,
    causal,
    kv,
    qt,
    gt,
    scores,
    low,
    acc,
    own,
    part,
    landed,
    totals,
    totals_ctx,
    totals_dp,
    kv_send,
    kv_recv,
    part_send,
    part_recv,
    ctx_send,
    ctx_recv,
    dp_send,
    dp_recv,
):
    head = pl.program_id(0)
    me = lax.axis_index("ctx")
    dp = lax.axis_index("dp")
    rows = k_in.shape[0]
    pairs = (me + 2) // 2

    def kv_copy(h, source, target):
        return pltpu.make_async_remote_copy(
            src_ref=kv.at[h, :, source],
            dst_ref=kv.at[h, :, source],
            send_sem=kv_send.at[h, target],
            recv_sem=kv_recv.at[h, source],
            device_id={"ctx": target},
            device_id_type=MESH,
        )

    def part_copy(h, sender, owner):
        return pltpu.make_async_remote_copy(
            src_ref=part.at[h, :, owner],
            dst_ref=landed.at[h, :, sender],
            send_sem=part_send.at[h, owner],
            recv_sem=part_recv.at[h, sender],
            device_id={"ctx": owner},
            device_id_type=MESH,
        )

    @pl.when(head == 0)
    def _():
        barrier = pltpu.get_barrier_semaphore()

        @pl.loop(1, ctx)
        def _(step):
            pl.semaphore_signal(
                barrier, inc=1, device_id={"ctx": lax.rem(me + step, ctx)}, device_id_type=MESH
            )

        @pl.loop(1, dps)
        def _(step):
            pl.semaphore_signal(
                barrier, inc=1, device_id={"dp": lax.rem(dp + step, dps)}, device_id_type=MESH
            )

        path = [me]
        depth = jnp.int32(0)
        for _ in range(ctx - 1):
            depth = depth + jnp.where(path[-1] != 0, 1, 0).astype(jnp.int32)
            path.append(parents[0, path[-1]])
        for block in range(ctx):
            seen = path[0] == block
            for node in path[1:]:
                seen = seen | (node == block)
            negs[block] = jnp.where(seen, jnp.float32(0.0), jnp.float32(NEG_LARGE))
        flat[...] = flat_table[depth]
        turned[...] = turned_table[depth]
        key_id = lax.broadcasted_iota(jnp.int32, (rows, rows), 0)
        row_id = lax.broadcasted_iota(jnp.int32, (rows, rows), 1)
        causal[...] = jnp.where(key_id <= row_id, 0.0, NEG_LARGE).astype(jnp.float32)
        for h in range(KV_HEADS):
            columns = pl.ds(h * HEAD, HEAD)
            x = k_in[:, columns].astype(jnp.float32) + k_bias[pl.ds(h, 1), :]
            x = x * flat[0] + pltpu.roll(x, HALF, 1) * flat[1]
            kv[h, 0, me] = x.astype(jnp.bfloat16)
            v = v_in[:, columns].astype(jnp.float32) + v_bias[pl.ds(h, 1), :]
            kv[h, 1, me] = v.astype(jnp.bfloat16)

        @pl.when(2 * pairs > me + 1)
        def _():
            for h in range(KV_HEADS):
                for which in range(2):
                    kv[h, which, me + 1] = jnp.zeros((rows, HEAD), jnp.bfloat16)

        pl.semaphore_wait(barrier, ctx + dps - 2)

        @pl.loop(0, KV_HEADS)
        def _(h):
            @pl.loop(0, ctx - 1 - me)
            def _(step):
                kv_copy(h, me, ctx - 1 - step).start()

    for g in range(GROUP):
        columns = pl.ds(g * HEAD, HEAD)
        x = (q_in[:, columns].astype(jnp.float32) + q_bias[pl.ds(g, 1), :]).T
        first, second = x[:HALF], x[HALF:]
        cosine, sine = turned[0] * LOG2_SCALE, turned[1] * LOG2_SCALE
        qt[pl.ds(0, HALF), columns] = (first * cosine - second * sine).astype(jnp.bfloat16)
        qt[pl.ds(HALF, HALF), columns] = (second * cosine + first * sine).astype(jnp.bfloat16)
        gt[:, columns] = g_in[:, columns].T

    @pl.loop(0, me)
    def _(source):
        kv_copy(head, source, me).wait_recv()

    def keys_of(which, pair):
        return kv[head, which, pl.ds(2 * pair, 2)].reshape(2 * rows, HEAD)

    wide = GROUP * rows

    def score_pair(pair, peak):
        tile = jnp.dot(keys_of(0, pair), qt[...], preferred_element_type=jnp.float32)
        for side in range(2):
            block = 2 * pair + side
            reach = jnp.where(block > me, NEG_LARGE, negs[jnp.minimum(block, ctx - 1)])
            mask = jnp.where(block == me, causal[...], reach)
            piece = tile[side * rows : (side + 1) * rows] + jnp.tile(mask, (1, GROUP))
            scores[pair, pl.ds(side * rows, rows), :] = piece
            peak = jnp.maximum(peak, jnp.max(piece, axis=0, keepdims=True))
        return peak

    peak = lax.fori_loop(
        0, pairs, score_pair, jnp.full((1, wide), NEG_LARGE, jnp.float32)
    )
    acc[...] = jnp.zeros_like(acc)

    def weigh_pair(pair, total):
        weights = jnp.exp2(scores[pair] - peak)
        rounded = weights.astype(jnp.bfloat16)
        low[pair] = rounded
        acc[...] += tn(keys_of(1, pair), rounded)
        return total + jnp.sum(weights, axis=0, keepdims=True)

    total = lax.fori_loop(0, pairs, weigh_pair, jnp.zeros((1, wide), jnp.float32))
    inverse = 1.0 / total
    attended = (acc[...] * inverse).astype(jnp.bfloat16)
    for g in range(GROUP):
        att_out[:, pl.ds(g * HEAD, HEAD)] = attended[:, g * HEAD : (g + 1) * HEAD].T
    grad = gt[...].astype(jnp.float32)
    delta = jnp.sum(grad * attended.astype(jnp.float32), axis=0, keepdims=True) * inverse
    gt[...] = (grad * inverse).astype(jnp.bfloat16)
    acc[...] = jnp.zeros_like(acc)

    @pl.loop(0, pairs)
    def _(pair):
        keys, values = keys_of(0, pair), keys_of(1, pair)
        rounded = low[pair]
        slopes = jnp.dot(values, gt[...], preferred_element_type=jnp.float32)
        steep = (rounded.astype(jnp.float32) * (slopes - delta)).astype(jnp.bfloat16)
        acc[...] += tn(keys, steep)
        key_part = nt(steep, qt[...]) * LN2
        value_part = nt(rounded, gt[...])
        for side in range(2):
            block = 2 * pair + side
            piece = slice(side * rows, (side + 1) * rows)

            @pl.when(block < me)
            def _():
                part[head, 0, block] = key_part[piece].astype(jnp.bfloat16)
                part[head, 1, block] = value_part[piece].astype(jnp.bfloat16)
                part_copy(head, me, block).start()

            @pl.when(block == me)
            def _():
                own[head, 0] = key_part[piece]
                own[head, 1] = value_part[piece]

    sums = []
    for g in range(GROUP):
        columns = pl.ds(g * HEAD, HEAD)
        x = acc[:, columns] * SCALE
        first, second = x[:HALF], x[HALF:]
        cosine, sine = turned[0], turned[1]
        back = jnp.concatenate(
            [first * cosine + second * sine, second * cosine - first * sine], axis=0
        ).T
        dq_out[:, columns] = back
        sums.append(jnp.sum(back, axis=0, keepdims=True))
    totals[pl.ds(pl.multiple_of(head * GROUP, GROUP), GROUP), :] = jnp.concatenate(sums, axis=0)

    @pl.when(head == KV_HEADS - 1)
    def _():
        for h in range(KV_HEADS):

            @pl.loop(me + 1, ctx)
            def _(sender):
                part_copy(h, sender, me).wait_recv()
                own[h] += landed[h, :, sender].astype(jnp.float32)

            x = own[h, 0]
            x = x * flat[0] - pltpu.roll(x, HALF, 1) * flat[1]
            columns = pl.ds(h * HEAD, HEAD)
            dk_out[:, columns] = x
            v = own[h, 1]
            dv_out[:, columns] = v
            totals[pl.ds(Q_HEADS + h, 1), :] = jnp.sum(x, axis=0, keepdims=True)
            totals[pl.ds(Q_HEADS + KV_HEADS + h, 1), :] = jnp.sum(v, axis=0, keepdims=True)

        def total_copy(axis, peer, slot, source, landing, send, recv):
            return pltpu.make_async_remote_copy(
                src_ref=source,
                dst_ref=landing.at[slot],
                send_sem=send.at[peer],
                recv_sem=recv.at[slot],
                device_id={axis: peer},
                device_id_type=MESH,
            )

        def exchange(axis, size, index, source, landing, send, recv):
            landing[index] = source[...]

            @pl.loop(1, size)
            def _(step):
                peer = lax.rem(index + step, size)
                total_copy(axis, peer, index, source, landing, send, recv).start()

            @pl.loop(1, size)
            def _(step):
                peer = lax.rem(index + step, size)
                total_copy(axis, peer, peer, source, landing, send, recv).wait_recv()

            result = landing[0]
            for slot in range(1, size):
                result = result + landing[slot]

            @pl.loop(1, size)
            def _(step):
                peer = lax.rem(index + step, size)
                total_copy(axis, peer, index, source, landing, send, recv).wait_send()

            return result

        totals[...] = exchange("ctx", ctx, me, totals, totals_ctx, ctx_send, ctx_recv)
        result = exchange("dp", dps, dp, totals, totals_dp, dp_send, dp_recv)
        qb_out[...] = result[:Q_HEADS]
        kb_out[...] = result[Q_HEADS : Q_HEADS + KV_HEADS]
        vb_out[...] = result[Q_HEADS + KV_HEADS :]

        @pl.loop(0, KV_HEADS)
        def _(h):
            @pl.loop(me + 1, ctx)
            def _(target):
                kv_copy(h, me, target).wait_send()

            @pl.loop(0, me)
            def _(owner):
                part_copy(h, me, owner).wait_send()


def body(query_input, key_input, value_input, out_grad, query_bias, key_bias, value_bias, parents):
    ctx, dps = lax.axis_size("ctx"), lax.axis_size("dp")
    _, rows, query_width = query_input.shape
    key_width = key_input.shape[2]
    flat_table, turned_table = tables(ctx, rows)
    f32, bf16 = jnp.float32, jnp.bfloat16
    whole = pl.BlockSpec(memory_space=pltpu.VMEM)
    wide = GROUP * rows
    group_block = pl.BlockSpec((rows, GROUP * HEAD), lambda h: (0, h))
    bias_rows = Q_HEADS + 2 * KV_HEADS
    dma = pltpu.SemaphoreType.DMA
    outs = pl.pallas_call(
        functools.partial(kernel, ctx, dps),
        grid=(KV_HEADS,),
        out_shape=(
            jax.ShapeDtypeStruct((rows, query_width), bf16),
            jax.ShapeDtypeStruct((rows, query_width), f32),
            jax.ShapeDtypeStruct((rows, key_width), f32),
            jax.ShapeDtypeStruct((rows, key_width), f32),
            jax.ShapeDtypeStruct((Q_HEADS, HEAD), f32),
            jax.ShapeDtypeStruct((KV_HEADS, HEAD), f32),
            jax.ShapeDtypeStruct((KV_HEADS, HEAD), f32),
        ),
        in_specs=[
            pl.BlockSpec(memory_space=pltpu.SMEM),
            group_block,
            whole,
            whole,
            group_block,
            pl.BlockSpec((GROUP, HEAD), lambda h: (h, 0)),
            whole,
            whole,
            whole,
            whole,
        ],
        out_specs=(group_block, group_block, whole, whole, whole, whole, whole),
        scratch_shapes=[
            pltpu.SMEM((ctx,), f32),
            pltpu.VMEM((2, rows, HEAD), f32),
            pltpu.VMEM((2, HALF, rows), f32),
            pltpu.VMEM((rows, rows), f32),
            pltpu.VMEM((KV_HEADS, 2, ctx, rows, HEAD), bf16),
            pltpu.VMEM((HEAD, wide), bf16),
            pltpu.VMEM((HEAD, wide), bf16),
            pltpu.VMEM((ctx // 2, 2 * rows, wide), f32),
            pltpu.VMEM((ctx // 2, 2 * rows, wide), bf16),
            pltpu.VMEM((HEAD, wide), f32),
            pltpu.VMEM((KV_HEADS, 2, rows, HEAD), f32),
            pltpu.VMEM((KV_HEADS, 2, ctx, rows, HEAD), bf16),
            pltpu.VMEM((KV_HEADS, 2, ctx, rows, HEAD), bf16),
            pltpu.VMEM((bias_rows, HEAD), f32),
            pltpu.VMEM((ctx, bias_rows, HEAD), f32),
            pltpu.VMEM((dps, bias_rows, HEAD), f32),
            dma((KV_HEADS, ctx)),
            dma((KV_HEADS, ctx)),
            dma((KV_HEADS, ctx)),
            dma((KV_HEADS, ctx)),
            dma((ctx,)),
            dma((ctx,)),
            dma((dps,)),
            dma((dps,)),
        ],
        compiler_params=pltpu.CompilerParams(
            collective_id=0,
            has_side_effects=True,
            vmem_limit_bytes=58 * 1024 * 1024,
            dimension_semantics=("arbitrary",),
        ),
    )(
        parents,
        query_input[0],
        key_input[0],
        value_input[0],
        out_grad[0],
        query_bias.reshape(Q_HEADS, HEAD),
        key_bias.reshape(KV_HEADS, HEAD),
        value_bias.reshape(KV_HEADS, HEAD),
        jnp.asarray(flat_table),
        jnp.asarray(turned_table),
    )
    attended, query_grad, key_grad, value_grad, query_total, key_total, value_total = outs
    return (
        attended[None],
        query_grad[None],
        key_grad[None],
        value_grad[None],
        query_total.reshape(-1),
        key_total.reshape(-1),
        value_total.reshape(-1),
    )


def solution(mesh):
    split = P("dp", "ctx", None)
    return jax.shard_map(
        body,
        mesh=mesh,
        in_specs=(split, split, split, split, P(), P(), P(), P("dp", None)),
        out_specs=(split, split, split, split, P(), P(), P()),
        check_vma=False,
    )
```

profile of v0, /device:TPU:0, one launch (start us, length us, event | category | flops | bytes accessed | tf_op | source)
XLA Modules:
  0.0 102.8 jit_solution(153618455423188813)
XLA Ops:
  0.6 93.5 %shard_map.153 = (bf16[128,8192]{1,0:T(8,128)(2,1)}, f32[128,8192]{1,0:T(8,128)}, f32[128,1024]{1,0:T(8,128)}, f32[128,1024]{1,0:T(8,128)}, f32[64,128]{1,0:T(8,...) custom-call(s32[1,8]{1,0:T(1,128)} %parents.1, bf16[128,8192]{1,0:T(8,128)(2,1)} %bitcast.15, bf16[128,1024]{1,0:T(8,128)(2,1)} %bitcast.20, ...), custom_call_target="tpu_custom_call" | custom-call | tf_op jit(solution)/shard_map/pallas_call | solution.py:336
  94.1 0.0 copy-start
  94.1 3.2 %copy.24 = bf16[1,128,8192]{2,1,0:T(8,128)(2,1)} copy(bf16[1,128,8192]{2,1,0:T(8,128)(2,1)} %bitcast.17) | data formatting | bytes 4194304
  97.4 0.0 copy-done
  97.4 0.0 copy-start.2
  97.4 0.0 copy-start.1
  97.4 2.0 %copy.25 = f32[1,128,8192]{2,1,0:T(8,128)} copy(f32[1,128,8192]{2,1,0:T(8,128)S(1)} %bitcast.14) | data formatting | bytes 8388608
  99.4 0.0 copy-done.2
  99.4 0.0 copy-start.3
  99.4 0.0 copy-start.5
  99.4 0.0 copy-start.4
  99.4 0.8 copy.26
  100.2 0.0 copy-done.1
  100.2 0.8 copy.27
  101.0 0.0 copy-done.3
  101.0 0.6 copy.28
  101.6 0.0 copy-done.5
  101.6 0.6 copy.29
  102.2 0.0 copy-done.4
  102.2 0.6 copy.30
Async XLA Ops:
  94.1 3.3 %copy-start = (f32[128,8192]{1,0:T(8,128)S(1)}, f32[128,8192]{1,0:T(8,128)}, u32[]{:S(2)}) copy-start(f32[128,8192]{1,0:T(8,128)} %get-tuple-element.15) | copy-start | bytes 12582916
  97.4 2.0 %copy-start.2 = (f32[128,1024]{1,0:T(8,128)S(1)}, f32[128,1024]{1,0:T(8,128)}, u32[]{:S(2)}) copy-start(f32[128,1024]{1,0:T(8,128)} %get-tuple-element.16) | copy-start | bytes 1572868
  97.4 2.8 %copy-start.1 = (f32[128,1024]{1,0:T(8,128)S(1)}, f32[128,1024]{1,0:T(8,128)}, u32[]{:S(2)}) copy-start(f32[128,1024]{1,0:T(8,128)} %get-tuple-element.17) | copy-start | bytes 1572868
  99.4 1.6 %copy-start.3 = (f32[64,128]{1,0:T(8,128)S(1)}, f32[64,128]{1,0:T(8,128)}, u32[]{:S(2)}) copy-start(f32[64,128]{1,0:T(8,128)} %get-tuple-element.18) | copy-start | bytes 98308
  99.4 2.2 %copy-start.5 = (f32[8,128]{1,0:T(8,128)S(1)}, f32[8,128]{1,0:T(8,128)}, u32[]{:S(2)}) copy-start(f32[8,128]{1,0:T(8,128)} %get-tuple-element.19) | copy-start | bytes 12292
  99.4 2.8 %copy-start.4 = (f32[8,128]{1,0:T(8,128)S(1)}, f32[8,128]{1,0:T(8,128)}, u32[]{:S(2)}) copy-start(f32[8,128]{1,0:T(8,128)} %get-tuple-element.20) | copy-start | bytes 12292
where the time goes:
time: 103 us
  Pallas kernels  93.5 us (91%)
  local copies, waits for them, and re-layouts  8.68 us (8%)
    pallas_call x1, Pallas kernels, body(): pl.pallas_call(functools.partial(kernel, ctx, dps), grid=(KV_HEADS,), out...  93.5 us
    unnamed x19, local copies, waits for them, and re-layouts  8.68 us

commit v1 on v0

--- a/solution.py
+++ b/solution.py
@@ -73,13 +73,16 @@
     acc,
     own,
     part,
+    pool,
     landed,
     totals,
     totals_ctx,
     totals_dp,
     kv_send,
     kv_recv,
+    relay_send,
     part_send,
+    pool_recv,
     part_recv,
     ctx_send,
     ctx_recv,
@@ -92,13 +95,40 @@
     rows = k_in.shape[0]
     pairs = (me + 2) // 2
 
-    def kv_copy(h, source, target):
+    chips = ctx // 2
+    chip, side_of = me // 2, lax.rem(me, 2)
+    sibling = me + 1 - 2 * side_of
+
+    def kv_copy(h, source, target, send_sem):
         return pltpu.make_async_remote_copy(
             src_ref=kv.at[h, :, source],
             dst_ref=kv.at[h, :, source],
-            send_sem=kv_send.at[h, target],
+            send_sem=send_sem,
             recv_sem=kv_recv.at[h, source],
             device_id={"ctx": target},
+            device_id_type=MESH,
+        )
+
+    def own_copy(h, target):
+        return kv_copy(h, me, target, kv_send.at[h, target])
+
+    def relay_copy(h, source):
+        return kv_copy(h, source, sibling, relay_send.at[h, source])
+
+    def relay(h):
+        @pl.loop(0, chip)
+        def _(other):
+            source = 2 * other + side_of
+            relay_copy(h, source).wait_recv()
+            relay_copy(h, source).start()
+
+    def pool_copy(h, block):
+        return pltpu.make_async_remote_copy(
+            src_ref=part.at[h, :, block],
+            dst_ref=pool.at[h, :, block // 2],
+            send_sem=part_send.at[h, block],
+            recv_sem=pool_recv.at[h, block // 2],
+            device_id={"ctx": sibling},
             device_id_type=MESH,
         )
 
@@ -111,6 +141,20 @@
             device_id={"ctx": owner},
             device_id_type=MESH,
         )
+
+    def combine(h):
+        @pl.loop(0, chip)
+        def _(other):
+            owner = 2 * other + side_of
+            pool_copy(h, owner).wait_recv()
+            summed = part[h, :, owner].astype(jnp.float32) + pool[h, :, other].astype(jnp.float32)
+            part[h, :, owner] = summed.astype(jnp.bfloat16)
+            part_copy(h, chip, owner).start()
+
+        @pl.when(side_of == 0)
+        def _():
+            pool_copy(h, me).wait_recv()
+            own[h] += pool[h, :, chip].astype(jnp.float32)
 
     @pl.when(head == 0)
     def _():
@@ -161,9 +205,15 @@
 
         @pl.loop(0, KV_HEADS)
         def _(h):
-            @pl.loop(0, ctx - 1 - me)
+            @pl.when(side_of == 0)
+            def _():
+                own_copy(h, sibling).start()
+
+            @pl.loop(0, chips - 1 - chip)
             def _(step):
-                kv_copy(h, me, ctx - 1 - step).start()
+                own_copy(h, 2 * (chips - 1 - step) + side_of).start()
+
+        relay(0)
 
     for g in range(GROUP):
         columns = pl.ds(g * HEAD, HEAD)
@@ -174,9 +224,10 @@
         qt[pl.ds(HALF, HALF), columns] = (second * cosine + first * sine).astype(jnp.bfloat16)
         gt[:, columns] = g_in[:, columns].T
 
-    @pl.loop(0, me)
-    def _(source):
-        kv_copy(head, source, me).wait_recv()
+    @pl.loop(0, chip + side_of)
+    def _(other):
+        source = 2 * other + 1 - side_of
+        relay_copy(head, source).wait_recv()
 
     def keys_of(which, pair):
         return kv[head, which, pl.ds(2 * pair, 2)].reshape(2 * rows, HEAD)
@@ -198,6 +249,14 @@
         0, pairs, score_pair, jnp.full((1, wide), NEG_LARGE, jnp.float32)
     )
     acc[...] = jnp.zeros_like(acc)
+
+    @pl.when(head < KV_HEADS - 1)
+    def _():
+        relay(head + 1)
+
+    @pl.when(head > 0)
+    def _():
+        combine(head - 1)
 
     def weigh_pair(pair, total):
         weights = jnp.exp2(scores[pair] - peak)
@@ -233,7 +292,10 @@
             def _():
                 part[head, 0, block] = key_part[piece].astype(jnp.bfloat16)
                 part[head, 1, block] = value_part[piece].astype(jnp.bfloat16)
-                part_copy(head, me, block).start()
+
+            @pl.when((block < me) & (side != side_of))
+            def _():
+                pool_copy(head, block).start()
 
             @pl.when(block == me)
             def _():
@@ -255,9 +317,10 @@
 
     @pl.when(head == KV_HEADS - 1)
     def _():
+        combine(KV_HEADS - 1)
         for h in range(KV_HEADS):
 
-            @pl.loop(me + 1, ctx)
+            @pl.loop(chip + 1, chips)
             def _(sender):
                 part_copy(h, sender, me).wait_recv()
                 own[h] += landed[h, :, sender].astype(jnp.float32)
@@ -313,13 +376,21 @@
 
         @pl.loop(0, KV_HEADS)
         def _(h):
-            @pl.loop(me + 1, ctx)
+            @pl.when(side_of == 0)
+            def _():
+                own_copy(h, sibling).wait_send()
+
+            @pl.loop(chip + 1, chips)
             def _(target):
-                kv_copy(h, me, target).wait_send()
+                own_copy(h, 2 * target + side_of).wait_send()
+
+            @pl.loop(0, chip)
+            def _(other):
+                relay_copy(h, 2 * other + side_of).wait_send()
 
             @pl.loop(0, me)
             def _(owner):
-                part_copy(h, me, owner).wait_send()
+                pool_copy(h, owner).wait_send()
 
 
 def body(query_input, key_input, value_input, out_grad, query_bias, key_bias, value_bias, parents):
@@ -371,7 +442,8 @@
             pltpu.VMEM((HEAD, wide), f32),
             pltpu.VMEM((KV_HEADS, 2, rows, HEAD), f32),
             pltpu.VMEM((KV_HEADS, 2, ctx, rows, HEAD), bf16),
-            pltpu.VMEM((KV_HEADS, 2, ctx, rows, HEAD), bf16),
+            pltpu.VMEM((KV_HEADS, 2, ctx // 2, rows, HEAD), bf16),
+            pltpu.VMEM((KV_HEADS, 2, ctx // 2, rows, HEAD), bf16),
             pltpu.VMEM((bias_rows, HEAD), f32),
             pltpu.VMEM((ctx, bias_rows, HEAD), f32),
             pltpu.VMEM((dps, bias_rows, HEAD), f32),
@@ -379,6 +451,8 @@
             dma((KV_HEADS, ctx)),
             dma((KV_HEADS, ctx)),
             dma((KV_HEADS, ctx)),
+            dma((KV_HEADS, ctx // 2)),
+            dma((KV_HEADS, ctx // 2)),
             dma((ctx,)),
             dma((ctx,)),
             dma((dps,)),

time: 103 us -> 95.4 us (0.926)
  Pallas kernels: 93.5 us -> 85.9 us
    pallas_call x1, Pallas kernels: 93.5 us -> 85.9 us  [body(): pl.pallas_call(functools.partial(kernel, ctx, dps), grid=(KV_HEADS,), out...]
where the time goes in v1:
time: 95.4 us; the launch traced here: 95.2 us
  Pallas kernels  85.9 us (90%)
  local copies, waits for them, and re-layouts  8.68 us (9%)
    pallas_call x1, Pallas kernels, body(): pl.pallas_call(functools.partial(kernel, ctx, dps), grid=(KV_HEADS,), out...  85.9 us
    unnamed x19, local copies, waits for them, and re-layouts  8.68 us

profile of v1, /device:TPU:0, one launch (start us, length us, event | category | flops | bytes accessed | tf_op | source)
XLA Modules:
  0.0 95.2 jit_solution(9827424107675763952)
XLA Ops:
  0.6 85.9 %shard_map.153 = (bf16[128,8192]{1,0:T(8,128)(2,1)}, f32[128,8192]{1,0:T(8,128)}, f32[128,1024]{1,0:T(8,128)}, f32[128,1024]{1,0:T(8,128)}, f32[64,128]{1,0:T(8,...) custom-call(s32[1,8]{1,0:T(1,128)} %parents.1, bf16[128,8192]{1,0:T(8,128)(2,1)} %bitcast.15, bf16[128,1024]{1,0:T(8,128)(2,1)} %bitcast.20, ...), custom_call_target="tpu_custom_call" | custom-call | tf_op jit(solution)/shard_map/pallas_call | solution.py:407
  86.6 0.0 copy-start
  86.6 3.2 %copy.24 = bf16[1,128,8192]{2,1,0:T(8,128)(2,1)} copy(bf16[1,128,8192]{2,1,0:T(8,128)(2,1)} %bitcast.17) | data formatting | bytes 4194304
  89.8 0.0 copy-done
  89.8 0.0 copy-start.2
  89.8 0.0 copy-start.1
  89.8 2.0 %copy.25 = f32[1,128,8192]{2,1,0:T(8,128)} copy(f32[1,128,8192]{2,1,0:T(8,128)S(1)} %bitcast.14) | data formatting | bytes 8388608
  91.8 0.0 copy-done.2
  91.8 0.0 copy-start.3
  91.8 0.0 copy-start.5
  91.8 0.0 copy-start.4
  91.8 0.8 copy.26
  92.6 0.0 copy-done.1
  92.6 0.8 copy.27
  93.4 0.0 copy-done.3
  93.4 0.6 copy.28
  94.1 0.0 copy-done.5
  94.1 0.6 copy.29
  94.7 0.0 copy-done.4
  94.7 0.6 copy.30
Async XLA Ops:
  86.6 3.3 %copy-start = (f32[128,8192]{1,0:T(8,128)S(1)}, f32[128,8192]{1,0:T(8,128)}, u32[]{:S(2)}) copy-start(f32[128,8192]{1,0:T(8,128)} %get-tuple-element.15) | copy-start | bytes 12582916
  89.8 2.0 %copy-start.2 = (f32[128,1024]{1,0:T(8,128)S(1)}, f32[128,1024]{1,0:T(8,128)}, u32[]{:S(2)}) copy-start(f32[128,1024]{1,0:T(8,128)} %get-tuple-element.16) | copy-start | bytes 1572868
  89.8 2.8 %copy-start.1 = (f32[128,1024]{1,0:T(8,128)S(1)}, f32[128,1024]{1,0:T(8,128)}, u32[]{:S(2)}) copy-start(f32[128,1024]{1,0:T(8,128)} %get-tuple-element.17) | copy-start | bytes 1572868
  91.8 1.6 %copy-start.3 = (f32[64,128]{1,0:T(8,128)S(1)}, f32[64,128]{1,0:T(8,128)}, u32[]{:S(2)}) copy-start(f32[64,128]{1,0:T(8,128)} %get-tuple-element.18) | copy-start | bytes 98308
  91.8 2.2 %copy-start.5 = (f32[8,128]{1,0:T(8,128)S(1)}, f32[8,128]{1,0:T(8,128)}, u32[]{:S(2)}) copy-start(f32[8,128]{1,0:T(8,128)} %get-tuple-element.19) | copy-start | bytes 12292
  91.8 2.8 %copy-start.4 = (f32[8,128]{1,0:T(8,128)S(1)}, f32[8,128]{1,0:T(8,128)}, u32[]{:S(2)}) copy-start(f32[8,128]{1,0:T(8,128)} %get-tuple-element.20) | copy-start | bytes 12292
